TPU v7x, 512 devices: a whole 4x4x16 slice. The times are simulated.
512 devices in a mesh: dp: 32 (over z_hi, y, x), shard: 16 (over z_lo, core).
Axes of the slice: x: 4, y: 4, z: 16 (z_hi: 2, z_lo: 8; z = z_hi * 8 + z_lo), core: 2. Of those that a mesh axis runs over, the one named last changes fastest.
Arguments:
- inputs: bfloat16 [8192, 8192], P('dp'), may hold values from -6 to 6
- cotangent: bfloat16 [2, 8192, 14336], P(None, 'dp', 'shard'), may hold values from -0.06591797 to 0.06591797
- subspace: bfloat16 [2, 8192, 256], P(None, 'dp'), may hold values from -0.0625 to 0.0625
- first_moment: float32 [2, 256, 14336], P(None, 'dp', 'shard'), may hold values from -2 to 2
- second_moment: float32 [2, 256, 14336], P(None, 'dp', 'shard'), may hold values from 0.0001 to 0.01
Outputs:
- update: bfloat16 [2, 8192, 14336], P(None, 'dp', 'shard')
- new_first: float32 [2, 256, 14336], P(None, 'dp', 'shard')
- new_second: float32 [2, 256, 14336], P(None, 'dp', 'shard')
All inputs are finite; a program needn't handle non-finite values.
Results may differ from a plain program's by a relative error of at most 0.0057.
Values may be sent and summed in bfloat16 or wider, within the bound.
No kernel may reach another device: no remote copies, remote signals or barrier semaphores. Data moves between devices by JAX's collectives and lax.ppermute only.
A program may use at most 64 MiB of HBM per device.

v0:
```python
import jax
import jax.numpy as jnp
from jax import lax
from jax.sharding import PartitionSpec as P

STEP = 10


def per_device(inputs, cotangent, subspace, first_moment, second_moment):
    projected = jnp.einsum(
        "td,gdr->gtr",
        inputs,
        lax.all_gather(subspace, "dp", axis=1, tiled=True),
        preferred_element_type=jnp.float32,
    ).astype(jnp.bfloat16)
    gathered_grad = lax.psum_scatter(
        jnp.einsum("gtr,gtc->rgc", projected, cotangent, preferred_element_type=jnp.float32),
        "dp",
        scatter_dimension=0,
        tiled=True,
    )
    gradient = jnp.transpose(gathered_grad, (1, 0, 2))
    new_first = 0.9 * first_moment + 0.1 * gradient
    new_second = 0.999 * second_moment + 0.001 * gradient * gradient
    first_fix = 1.0 - 0.9**STEP
    second_fix = 1.0 - 0.999**STEP
    normalized = (new_first / first_fix / (jnp.sqrt(new_second / second_fix) + 1e-08)).astype(
        jnp.bfloat16
    )
    update = jnp.einsum(
        "gdr,grc->gdc",
        subspace,
        lax.all_gather(normalized, "dp", axis=1, tiled=True),
        preferred_element_type=jnp.float32,
    ).astype(jnp.bfloat16)
    return (update, new_first, new_second)


def solution(mesh):
    return jax.shard_map(
        per_device,
        mesh=mesh,
        in_specs=(
            P("dp", None),
            P(None, "dp", "shard"),
            P(None, "dp", None),
            P(None, "dp", "shard"),
            P(None, "dp", "shard"),
        ),
        out_specs=(P(None, "dp", "shard"), P(None, "dp", "shard"), P(None, "dp", "shard")),
        check_vma=False,
    )
```

profile of v0, /device:TPU:2, one launch (start us, length us, event | category | flops | bytes accessed | tf_op | source)
XLA Modules:
  0.0 745.6 jit_solution(13376802077764518758)
XLA Ops:
  7.2 0.0 copy-start
  7.2 0.0 all-gather.2.cloned.1.call-start
  7.2 0.7 all-gather.2.cloned.1.call-update
  7.9 0.0 copy-start.2
  7.9 0.0 copy-start.3
  7.9 0.0 copy-start.1
  7.9 0.0 reduce-scatter.2.cloned.1.call-start
  8.0 254.5 %all-gather.2.cloned.1.call-done = bf16[2,8192,256]{2,1,0:T(8,128)(2,1)} async-done(((bf16[2,256,256]{2,1,0:T(8,128)(2,1)}), bf16[2,8192,256]{2,1,0:T(8,128)(2,1)}) %all-gather.2.cloned.1.call-update) | async-done | bytes 8388624 | tf_op jit(solution)/shard_map/all_gather | solution.py:13
  262.5 0.0 copy-done
  262.5 9.0 %convolution_bitcast_fusion = f32[256,2,896]{2,0,1:T(8,128)} fusion(bf16[2,256,896]{2,1,0:T(8,128)(2,1)S(1)} %copy-done, bf16[2,8192,256]{2,1,0:T(8,128)(2,1)} %all-gather.2.cloned.1.call-done, bf16[256,8192]{1,0:T(8,128)(2,1)} %param.5), kind=kOutput, calls=%fused_computation.2 | convolution fusion | flops 2382495744 | bytes 15335424 | tf_op jit(solution)/shard_map/gtr,gtc->rgc/dot_general | solution.py:17
  271.5 0.0 reduce-scatter.2.cloned.1.call-update
  271.5 298.1 %reduce-scatter.2.cloned.1.call-done = f32[8,2,896]{2,0,1:T(8,128)} async-done(((f32[256,2,896]{2,0,1:T(8,128)}), f32[8,2,896]{2,0,1:T(8,128)}) %reduce-scatter.2.cloned.1.call-update) | async-done | bytes 57360 | tf_op jit(solution)/shard_map/reduce_scatter | solution.py:16
  569.6 0.0 copy-done.2
  569.6 0.0 copy-done.3
  569.6 1.5 divide_convert_fusion
  571.1 165.9 %all_gather.7 = bf16[2,256,896]{2,1,0:T(8,128)(2,1)S(1)} all-gather(bf16[2,8,896]{2,1,0:T(8,128)(2,1)S(1)} %get-tuple-element.6), channel_id=1, replica_groups=mesh['dp'=32,'shard'=16] {'dp'}, dimensions={1}, use_global_device_ids=true | all-gather | bytes 946176 | tf_op jit(solution)/shard_map/all_gather | solution.py:33
  737.0 0.0 copy-done.1
  737.0 0.5 fusion.2
  737.5 1.3 copy.8
Async XLA Ops:
  7.2 255.3 %copy-start = (bf16[2,256,896]{2,1,0:T(8,128)(2,1)S(1)}, bf16[2,256,896]{2,1,0:T(8,128)(2,1)}, u32[]{:S(2)}) copy-start(bf16[2,256,896]{2,1,0:T(8,128)(2,1)} %param.6) | copy-start | bytes 2752516
  7.2 255.3 %all-gather.2.cloned.1.call-start = ((), (), s32[]{:S(2)}) async-start(), calls=%async_computation.1 | async-start | bytes 8650752 | tf_op jit(solution)/shard_map/all_gather | solution.py:13
  7.9 561.7 %copy-start.2 = (f32[2,8,896]{2,1,0:T(8,128)S(1)}, f32[2,8,896]{2,1,0:T(8,128)}, u32[]{:S(2)}) copy-start(f32[2,8,896]{2,1,0:T(8,128)} %param.8) | copy-start | bytes 172036
  7.9 561.7 %copy-start.3 = (f32[2,8,896]{2,1,0:T(8,128)S(1)}, f32[2,8,896]{2,1,0:T(8,128)}, u32[]{:S(2)}) copy-start(f32[2,8,896]{2,1,0:T(8,128)} %param.9) | copy-start | bytes 172036
  7.9 729.0 %copy-start.1 = (bf16[2,256,256]{2,1,0:T(8,128)(2,1)S(1)}, bf16[2,256,256]{2,1,0:T(8,128)(2,1)}, u32[]{:S(2)}) copy-start(bf16[2,256,256]{2,1,0:T(8,128)(2,1)} %param.7) | copy-start | bytes 786436
  7.9 561.7 %reduce-scatter.2.cloned.1.call-start = ((), (), s32[]{:S(2)}) async-start(), calls=%async_computation.2 | async-start | bytes 1892352 | tf_op jit(solution)/shard_map/reduce_scatter | solution.py:16
Sparse Core Ops, SparseCore 0:
  12.4 250.0 all-gather.1
  271.6 297.9 reduce-scatter.1
where the time goes:
time: 746 us
  waiting for transfers between devices  553 us (74%)
  blocking collectives  166 us (22%)
  between operations  14.1 us (2%)
  matrix products  9.5 us (1%)
    reduce_scatter x1, waiting for transfers between devices, per_device(): lax.psum_scatter(jnp.einsum('gtr,gtc->rgc', projected, cotangent, preferr...  298 us
    all_gather x1, waiting for transfers between devices, per_device(): lax.all_gather(subspace, 'dp', axis=1, tiled=True)  255 us
    all_gather x1, blocking collectives, per_device(): lax.all_gather(normalized, 'dp', axis=1, tiled=True)  166 us
  transfers between devices with their start and end apart: 2, of which 2 were waited for; matrix products, arithmetic and copies ran while one was open for 0% of the time, Pallas kernels for 0%

commit v1 on v0

v1 whole, which is shorter than its diff:
```python
import jax
import jax.numpy as jnp
from jax import lax
from jax.sharding import Mesh, PartitionSpec as P

STEP = 10
PLANE = ("y", "x")
LINE = ("zl", "c")


def per_device(inputs, cotangent, subspace, first_moment, second_moment):
    f32, bf16 = jnp.float32, jnp.bfloat16
    swap = [(0, 1), (1, 0)]
    moments = jnp.stack([first_moment, second_moment])
    moments_far = lax.ppermute(moments, "zh", swap)

    ranks = subspace.reshape(2, 256, 2, 16, 8).transpose(3, 0, 2, 4, 1)
    place = lax.axis_index(LINE)
    mine = lax.dynamic_index_in_dim(ranks, place, 0, keepdims=False).reshape(32, 256)
    other = lax.ppermute(mine, "zh", swap)
    half = lax.axis_index("zh")
    both = jnp.where(half == 0, jnp.stack([mine, other]), jnp.stack([other, mine]))
    basis = lax.all_to_all(
        jnp.broadcast_to(both, (16, 2, 32, 256)), PLANE, 0, 0, tiled=True
    )
    basis = basis.transpose(2, 1, 0, 3).reshape(32, 8192)
    projected = lax.dot_general(
        basis, inputs, (((1,), (1,)), ((), ())), preferred_element_type=f32
    ).astype(bf16)
    projected = lax.all_to_all(
        jnp.broadcast_to(projected, (8, 32, 256)), "zl", 0, 0, tiled=True
    )
    projected = lax.all_gather(projected, "c", axis=1).reshape(16, 2, 2, 8, 256)
    partial = jnp.einsum(
        "yghkt,gtc->yghkc", projected, cotangent, preferred_element_type=f32
    ).astype(bf16)
    parts = lax.all_to_all(partial, PLANE, 0, 0, tiled=True)
    own = jnp.sum(parts.astype(f32), axis=0)
    far = lax.ppermute(own.astype(bf16), "zh", swap)
    gradient = own + far.astype(f32)

    near_far = jnp.stack([moments, moments_far], axis=2)
    far_near = jnp.stack([moments_far, moments], axis=2)
    held = jnp.where(half == 0, near_far, far_near)
    new_first = 0.9 * held[0] + 0.1 * gradient
    new_second = 0.999 * held[1] + 0.001 * gradient * gradient
    first_fix = 1.0 - 0.9**STEP
    second_fix = 1.0 - 0.999**STEP
    normalized = (new_first / first_fix / (jnp.sqrt(new_second / second_fix) + 1e-08)).astype(bf16)
    steps = lax.all_to_all(
        jnp.broadcast_to(normalized, (16, 2, 2, 8, 896)), PLANE, 0, 0, tiled=True
    )
    update = jnp.einsum(
        "yghkd,yghkc->gdc", ranks, steps, preferred_element_type=f32
    ).astype(bf16)
    return (
        update,
        jnp.where(half == 0, new_first[:, 0], new_first[:, 1]),
        jnp.where(half == 0, new_second[:, 0], new_second[:, 1]),
    )


def solution(mesh):
    fine = Mesh(mesh.devices.reshape(2, 4, 4, 8, 2), ("zh", "y", "x", "zl", "c"))
    dp, shard = ("zh", "y", "x"), ("zl", "c")
    return jax.shard_map(
        per_device,
        mesh=fine,
        in_specs=(
            P(dp, None),
            P(None, dp, shard),
            P(None, dp, None),
            P(None, dp, shard),
            P(None, dp, shard),
        ),
        out_specs=(P(None, dp, shard), P(None, dp, shard), P(None, dp, shard)),
        check_vma=False,
    )
```

time: 746 us -> 126 us (0.17)
  the two profiles are of different devices: /device:TPU:2 before, /device:TPU:1 now
where the time goes in v1:
time: 126 us; the launch traced here: 125 us
  starting transfers between devices  43.9 us (35%)
  blocking collectives  41.1 us (33%)
  waiting for transfers between devices  28.5 us (23%)
  local copies, waits for them, and re-layouts  5.65 us (4%)
  matrix products  4.47 us (4%)
    all_to_all x1, blocking collectives, per_device(): lax.all_to_all(jnp.broadcast_to(projected, (8, 32, 256)), 'zl', 0, 0, til...  18.4 us
    all_to_all x1, blocking collectives, per_device(): lax.all_to_all(jnp.broadcast_to(both, (16, 2, 32, 256)), PLANE, 0, 0, til...  16.6 us
    ppermute x1, starting transfers between devices, per_device(): other = lax.ppermute(mine, 'zh', swap)  16.3 us
    all_to_all x1, waiting for transfers between devices, per_device(): lax.all_to_all(jnp.broadcast_to(normalized, (16, 2, 2, 8, 896)), PLANE, 0...  14.1 us
    all_to_all x1, starting transfers between devices, per_device(): lax.all_to_all(jnp.broadcast_to(normalized, (16, 2, 2, 8, 896)), PLANE, 0...  8.06 us
    ppermute x1, starting transfers between devices, per_device(): moments_far = lax.ppermute(moments, 'zh', swap)  7.94 us
    ppermute x1, starting transfers between devices, per_device(): far = lax.ppermute(own.astype(bf16), 'zh', swap)  7.94 us
    all_to_all x1, waiting for transfers between devices, per_device(): parts = lax.all_to_all(partial, PLANE, 0, 0, tiled=True)  7.51 us
  transfers between devices with their start and end apart: 5, of which 4 were waited for; matrix products, arithmetic and copies ran while one was open for 1% of the time, Pallas kernels for 0%

profile of v1, /device:TPU:1, one launch (start us, length us, event | category | flops | bytes accessed | tf_op | source)
XLA Modules:
  0.0 125.4 jit_solution(4362996449960066750)
XLA Ops:
  0.7 1.2 copy.17
  1.8 16.3 %collective-permute-start.1 = (bf16[32,256]{1,0:T(8,128)(2,1)S(1)}, bf16[32,256]{1,0:T(8,128)(2,1)S(1)}, u32[]{:S(2)}, u32[]{:S(2)}) collective-permute-start(bf16[32,256]{1,0:T(8,128)(2,1)S(1)} %bitcast.58), channel_id=1, source_target_pairs={{0,256},{256,0},{1,257},{257,1},{2,258},{258,2},{3,259},{259,3},{4... | collective-permute-start | bytes 49160 | tf_op jit(solution)/shard_map/ppermute | solution.py:20
  18.1 1.2 collective-permute-done.1
  19.4 0.4 broadcast_in_dim.9
  19.8 16.6 %all_to_all.20 = bf16[16,2,32,256]{3,1,2,0:T(2,128)(2,1)S(1)} all-to-all(bf16[16,2,32,256]{3,1,2,0:T(2,128)(2,1)S(1)} %broadcast_in_dim.9), channel_id=1, replica_groups=mesh['zh'=2,'y'=4,'x'=4,'zl'=8,'c'=2] {'y','x'}, dimensions={0} | all-to-all | bytes 1048576 | tf_op jit(solution)/shard_map/all_to_all | solution.py:23
  36.4 0.4 copy.19
  36.9 0.3 copy.32
  37.2 3.5 %convolution_convert_fusion.1 = bf16[32,256]{1,0:T(8,128)(2,1)S(1)} fusion(bf16[32,8192]{1,0:T(8,128)(2,1)S(1)} %bitcast.51, bf16[256,8192]{1,0:T(8,128)(2,1)} %param.5), kind=kOutput, calls=%fused_computation.5 | convolution fusion | flops 134225920 | bytes 4734976 | tf_op jit(solution)/shard_map/dot_general | solution.py:27
  40.8 18.4 %all_to_all.21 = bf16[8,32,256]{2,1,0:T(8,128)(2,1)S(1)} all-to-all(bf16[8,32,256]{2,1,0:T(8,128)(2,1)S(1)} %broadcast_in_dim.10), channel_id=1, replica_groups=mesh['zh'=2,'y'=4,'x'=4,'zl'=8,'c'=2] {'zl'}, dimensions={0} | all-to-all | bytes 262144 | tf_op jit(solution)/shard_map/all_to_all | solution.py:30
  59.2 6.1 %all-gather = bf16[8,64,256]{2,1,0:T(8,128)(2,1)S(1)} all-gather(bf16[8,32,256]{2,1,0:T(8,128)(2,1)S(1)} %all_to_all.21), channel_id=2, replica_groups=mesh['zh'=2,'y'=4,'x'=4,'zl'=8,'c'=2] {'c'}, dimensions={1}, use_global_device_ids=true | all-gather | bytes 393216 | tf_op jit(solution)/shard_map/all_gather | solution.py:33
  65.3 0.4 fusion
  65.7 1.0 copy.21
  66.7 3.6 %all-to-all-start.2 = ((bf16[16,2,2,8,896]{4,3,2,1,0:T(8,128)(2,1)}), bf16[16,2,2,8,896]{4,3,2,1,0:T(8,128)(2,1)S(1)}, u32[]{:S(2)}, u32[]{:S(2)}) async-start(bf16[16,2,2,8,896]{4,3,2,1,0:T(8,128)(2,1)} %copy.21), calls=%async_computation.2 | async-start | bytes 1835008 | tf_op jit(solution)/shard_map/all_to_all | solution.py:37
  70.4 7.9 %collective-permute-start = (f32[2,2,8,896]{3,2,1,0:T(8,128)S(1)}, f32[2,2,8,896]{3,2,1,0:T(8,128)S(1)}, u32[]{:S(2)}, u32[]{:S(2)}) collective-permute-start(f32[2,2,8,896]{3,2,1,0:T(8,128)S(1)} %get-tuple-element.16), channel_id=1, source_target_pairs={{0,256},{256,0},{1,257},{257,1},{2,258},{258,2},{3,259},{259,3},{4... | collective-permute-start | bytes 344072 | tf_op jit(solution)/shard_map/ppermute | solution.py:15
  78.3 7.5 %all-to-all-done.2 = bf16[16,2,2,8,896]{4,3,2,1,0:T(8,128)(2,1)S(1)} async-done(((bf16[16,2,2,8,896]{4,3,2,1,0:T(8,128)(2,1)}), bf16[16,2,2,8,896]{4,3,2,1,0:T(8,128)(2,1)S(1)}, u32[]{:S(2)}, u32[]{:S(2)}) %all-to-all-start.2) | async-done | bytes 917536 | tf_op jit(solution)/shard_map/all_to_all | solution.py:37
  85.9 0.1 convert_reduce_fusion
  86.0 7.9 %collective-permute-start.2 = (bf16[2,2,8,896]{3,2,1,0:T(8,128)(2,1)S(1)}, bf16[2,2,8,896]{3,2,1,0:T(8,128)(2,1)S(1)}, u32[]{:S(2)}, u32[]{:S(2)}) collective-permute-start(bf16[2,2,8,896]{3,2,1,0:T(8,128)(2,1)S(1)} %convert_element_type.31), channel_id=1, source_target_pairs={{0,256},{256,0},{1,257},{257,1},{2,258},{258,2},{3,259},{259,3},{4... | collective-permute-start | bytes 172040 | tf_op jit(solution)/shard_map/ppermute | solution.py:39
  94.0 5.7 %collective-permute-done.2 = bf16[2,2,8,896]{3,2,1,0:T(8,128)(2,1)S(1)} collective-permute-done((bf16[2,2,8,896]{3,2,1,0:T(8,128)(2,1)S(1)}, bf16[2,2,8,896]{3,2,1,0:T(8,128)(2,1)S(1)}, u32[]{:S(2)}, u32[]{:S(2)}) %collective-permute-start.2) | collective-permute-done | bytes 57376 | tf_op jit(solution)/shard_map/ppermute | solution.py:39
  99.8 1.0 broadcast_in_dim.11
  100.8 8.1 %all-to-all-start.3 = ((bf16[16,2,2,8,896]{4,3,2,1,0:T(8,128)(2,1)}), bf16[16,2,2,8,896]{4,3,2,1,0:T(8,128)(2,1)S(1)}, u32[]{:S(2)}, u32[]{:S(2)}) async-start(bf16[16,2,2,8,896]{4,3,2,1,0:T(8,128)(2,1)} %broadcast_in_dim.11), calls=%async_computation.3 | async-start | bytes 1835008 | tf_op jit(solution)/shard_map/all_to_all | solution.py:50
  108.8 0.7 fusion.9
  109.5 14.1 %all-to-all-done.3 = bf16[16,2,2,8,896]{4,3,2,1,0:T(8,128)(2,1)S(1)} async-done(((bf16[16,2,2,8,896]{4,3,2,1,0:T(8,128)(2,1)}), bf16[16,2,2,8,896]{4,3,2,1,0:T(8,128)(2,1)S(1)}, u32[]{:S(2)}, u32[]{:S(2)}) %all-to-all-start.3) | async-done | bytes 917536 | tf_op jit(solution)/shard_map/all_to_all | solution.py:50
  123.6 0.5 fusion.1
  124.1 1.3 %copy.25 = bf16[2,256,896]{2,1,0:T(8,128)(2,1)} copy(bf16[2,256,896]{1,2,0:T(8,128)(2,1)S(1)} %fusion.1) | data formatting | bytes 1835008
  (15 shorter events, 0.2 us)
Async XLA Ops:
  0.6 64.6 %copy-start = (bf16[2,256,896]{2,1,0:T(8,128)(2,1)S(1)}, bf16[2,256,896]{2,1,0:T(8,128)(2,1)}, u32[]{:S(2)}) copy-start(bf16[2,256,896]{2,1,0:T(8,128)(2,1)} %param.6) | copy-start | bytes 2752516
  1.8 17.5 %collective-permute-start.1 = (bf16[32,256]{1,0:T(8,128)(2,1)S(1)}, bf16[32,256]{1,0:T(8,128)(2,1)S(1)}, u32[]{:S(2)}, u32[]{:S(2)}) collective-permute-start(bf16[32,256]{1,0:T(8,128)(2,1)S(1)} %bitcast.58), channel_id=1, source_target_pairs={{0,256},{256,0},{1,257},{257,1},{2,258},{258,2},{3,259},{259,3},{4... | collective-permute-start | bytes 49160 | tf_op jit(solution)/shard_map/ppermute | solution.py:20
  40.7 29.6 %copy-start.1 = (f32[2,8,896]{2,1,0:T(8,128)S(1)}, f32[2,8,896]{2,1,0:T(8,128)}, u32[]{:S(2)}) copy-start(f32[2,8,896]{2,1,0:T(8,128)} %param.9) | copy-start | bytes 172036
  40.7 29.6 %copy-start.2 = (f32[2,8,896]{2,1,0:T(8,128)S(1)}, f32[2,8,896]{2,1,0:T(8,128)}, u32[]{:S(2)}) copy-start(f32[2,8,896]{2,1,0:T(8,128)} %param.8) | copy-start | bytes 172036
  66.7 19.2 %all-to-all-start.2 = ((bf16[16,2,2,8,896]{4,3,2,1,0:T(8,128)(2,1)}), bf16[16,2,2,8,896]{4,3,2,1,0:T(8,128)(2,1)S(1)}, u32[]{:S(2)}, u32[]{:S(2)}) async-start(bf16[16,2,2,8,896]{4,3,2,1,0:T(8,128)(2,1)} %copy.21), calls=%async_computation.2 | async-start | bytes 1835008 | tf_op jit(solution)/shard_map/all_to_all | solution.py:37
  70.4 23.6 %collective-permute-start = (f32[2,2,8,896]{3,2,1,0:T(8,128)S(1)}, f32[2,2,8,896]{3,2,1,0:T(8,128)S(1)}, u32[]{:S(2)}, u32[]{:S(2)}) collective-permute-start(f32[2,2,8,896]{3,2,1,0:T(8,128)S(1)} %get-tuple-element.16), channel_id=1, source_target_pairs={{0,256},{256,0},{1,257},{257,1},{2,258},{258,2},{3,259},{259,3},{4... | collective-permute-start | bytes 344072 | tf_op jit(solution)/shard_map/ppermute | solution.py:15
  86.0 13.7 %collective-permute-start.2 = (bf16[2,2,8,896]{3,2,1,0:T(8,128)(2,1)S(1)}, bf16[2,2,8,896]{3,2,1,0:T(8,128)(2,1)S(1)}, u32[]{:S(2)}, u32[]{:S(2)}) collective-permute-start(bf16[2,2,8,896]{3,2,1,0:T(8,128)(2,1)S(1)} %convert_element_type.31), channel_id=1, source_target_pairs={{0,256},{256,0},{1,257},{257,1},{2,258},{258,2},{3,259},{259,3},{4... | collective-permute-start | bytes 172040 | tf_op jit(solution)/shard_map/ppermute | solution.py:39
  100.8 22.9 %all-to-all-start.3 = ((bf16[16,2,2,8,896]{4,3,2,1,0:T(8,128)(2,1)}), bf16[16,2,2,8,896]{4,3,2,1,0:T(8,128)(2,1)S(1)}, u32[]{:S(2)}, u32[]{:S(2)}) async-start(bf16[16,2,2,8,896]{4,3,2,1,0:T(8,128)(2,1)} %broadcast_in_dim.11), calls=%async_computation.3 | async-start | bytes 1835008 | tf_op jit(solution)/shard_map/all_to_all | solution.py:50

commit v2 on v1

v2 whole, which is shorter than its diff:
```python
import jax
import jax.numpy as jnp
from jax import lax
from jax.experimental import pallas as pl
from jax.experimental.pallas import tpu as pltpu
from jax.sharding import Mesh, PartitionSpec as P

STEP = 10
PLANE = ("y", "x")
LINE = ("z_hi", "z_top", "z_mid", "z_lo")
NEAR = ("z_mid", "z_lo")
SWAP = [(0, 1), (1, 0)]
f32, bf16 = jnp.float32, jnp.bfloat16


def spread(block, axes, count):
    return lax.all_to_all(
        jnp.broadcast_to(block, (count, *block.shape)), axes, 0, 0, tiled=True
    )


def in_vmem(kernel, out, name, *operands):
    spec = pl.BlockSpec(memory_space=pltpu.VMEM)
    return pl.pallas_call(
        kernel,
        in_specs=[spec] * len(operands),
        out_specs=jax.tree.map(lambda _: spec, out),
        out_shape=out,
        compiler_params=pltpu.CompilerParams(vmem_limit_bytes=16 * 2**20),
        name=name,
    )(*operands)


def fetch_kernel(column_ref, inputs_ref, out_ref, sem):
    column = pl.multiple_of(column_ref[0], 4096)
    copy = pltpu.make_async_copy(inputs_ref.at[:, pl.ds(column, 4096)], out_ref, sem)
    copy.start()
    copy.wait()


def fetch(inputs, column):
    return pl.pallas_call(
        fetch_kernel,
        in_specs=[
            pl.BlockSpec(memory_space=pltpu.SMEM),
            pl.BlockSpec(memory_space=pl.ANY),
        ],
        out_specs=pl.BlockSpec(memory_space=pltpu.VMEM),
        out_shape=jax.ShapeDtypeStruct((256, 4096), bf16),
        scratch_shapes=[pltpu.SemaphoreType.DMA],
        compiler_params=pltpu.CompilerParams(vmem_limit_bytes=16 * 2**20),
        name="fetch",
    )(column.reshape(1), inputs)


def project_kernel(basis_ref, inputs_ref, out_ref):
    acc = jnp.zeros((256, 128), f32)
    for place in range(16):
        acc += jnp.dot(
            inputs_ref[:, place * 256 : (place + 1) * 256],
            basis_ref[place],
            preferred_element_type=f32,
        )
    out_ref[...] = jnp.broadcast_to(acc.T.astype(bf16), (4, 128, 256))


def gradient_kernel(halves_ref, cotangent_ref, out_ref):
    for g in range(2):
        both = halves_ref[g, 0].astype(f32) + halves_ref[g, 1].astype(f32)
        part = jnp.dot(both.astype(bf16), cotangent_ref[g], preferred_element_type=f32)
        out_ref[:, g] = part.astype(bf16).reshape(16, 16, 896)


def update_kernel(basis_ref, steps_ref, gradient_ref, first_ref, second_ref, *refs):
    outs, (update, first, second, sems) = refs[:3], refs[3:]
    gradient = gradient_ref[...]
    first[...] = 0.9 * first_ref[...] + 0.1 * gradient
    second[...] = 0.999 * second_ref[...] + 0.001 * gradient * gradient
    copies = [
        pltpu.make_async_copy(first, outs[1], sems.at[2]),
        pltpu.make_async_copy(second, outs[2], sems.at[3]),
    ]
    for copy in copies:
        copy.start()
    for g in range(2):
        steps = steps_ref[:, g].reshape(256, 896)
        update[g] = jnp.dot(basis_ref[g], steps, preferred_element_type=f32).astype(bf16)
        copies.append(pltpu.make_async_copy(update.at[g], outs[0].at[g], sems.at[g]))
        copies[-1].start()
    for copy in copies:
        copy.wait()


def finish(basis, steps, gradient, first_moment, second_moment):
    outs = (
        jax.ShapeDtypeStruct((2, 256, 896), bf16),
        jax.ShapeDtypeStruct((2, 8, 896), f32),
        jax.ShapeDtypeStruct((2, 8, 896), f32),
    )
    return pl.pallas_call(
        update_kernel,
        in_specs=[pl.BlockSpec(memory_space=pltpu.VMEM)] * 5,
        out_specs=(pl.BlockSpec(memory_space=pl.ANY),) * 3,
        out_shape=outs,
        scratch_shapes=[
            *(pltpu.VMEM(out.shape, out.dtype) for out in outs),
            pltpu.SemaphoreType.DMA((4,)),
        ],
        compiler_params=pltpu.CompilerParams(vmem_limit_bytes=16 * 2**20),
        name="finish",
    )(basis, steps, gradient, first_moment, second_moment)


def per_device(inputs, cotangent, subspace, first_moment, second_moment):
    half, core = lax.axis_index("z_hi"), lax.axis_index("core")
    low = lax.axis_index("z_lo")
    across = lax.axis_index("z_mid") == lax.axis_index("z_top")

    order = lax.broadcasted_iota(jnp.int32, (256,), 0)
    order = order // 8 % 2 * 128 + order // 16 * 8 + order % 8
    wanted = lax.dynamic_slice(order, (jnp.where(across, 1 - low, low) * 128,), (128,))
    every = lax.broadcasted_iota(jnp.int32, (128, 256), 1)
    pick = (wanted[:, None] == every).astype(bf16)
    chosen = lax.dynamic_index_in_dim(subspace, core, 0, keepdims=False)
    mine = jnp.einsum("dr,sr->ds", chosen, pick, preferred_element_type=f32).astype(bf16)
    theirs = lax.ppermute(mine, LINE, [(z, 15 - z) for z in (0, 1, 6, 7, 8, 9, 14, 15)])
    moments = jnp.stack([first_moment, second_moment])
    moments_far = lax.ppermute(moments, "z_hi", SWAP)
    features = jnp.where(across, 1 - half, half) * 4096
    held = fetch(inputs, features)
    basis = jnp.where(across, theirs, mine)
    basis, held = lax.optimization_barrier((basis, held))

    basis = spread(basis, PLANE, 16)
    projected = in_vmem(
        project_kernel, jax.ShapeDtypeStruct((4, 128, 256), bf16), "project", basis, held
    )
    projected = lax.all_to_all(projected, NEAR, 0, 0, tiled=True)
    projected = lax.all_gather(projected, "core", axis=0).reshape(2, 2, 256, 256)
    partial = in_vmem(
        gradient_kernel,
        jax.ShapeDtypeStruct((16, 2, 16, 896), bf16),
        "gradient_parts",
        projected,
        cotangent,
    )
    parts = lax.all_to_all(partial, PLANE, 0, 0, tiled=True)
    own = jnp.sum(parts.astype(f32), axis=0).reshape(2, 2, 8, 896)
    far = lax.ppermute(own.astype(bf16), "z_hi", SWAP)
    after, _ = lax.optimization_barrier((subspace, own))
    move = (order[:, None] == lax.broadcasted_iota(jnp.int32, (256, 256), 1)).astype(bf16)
    ordered = jnp.einsum("gdr,sr->gds", after, move, preferred_element_type=f32).astype(bf16)
    gradient = own + far.astype(f32)

    near_far = jnp.stack([moments, moments_far], axis=2)
    far_near = jnp.stack([moments_far, moments], axis=2)
    held = jnp.where(half == 0, near_far, far_near)
    first_fix = 1.0 - 0.9**STEP
    second_fix = 1.0 - 0.999**STEP
    new_first = 0.9 * held[0] + 0.1 * gradient
    new_second = 0.999 * held[1] + 0.001 * gradient * gradient
    normalized = new_first / first_fix / (jnp.sqrt(new_second / second_fix) + 1e-08)
    gradient = lax.dynamic_index_in_dim(gradient, half, 1, keepdims=False)
    normalized, gradient, ordered = lax.optimization_barrier(
        (normalized.astype(bf16).reshape(2, 16, 896), gradient, ordered)
    )
    steps = spread(normalized, PLANE, 16)
    return finish(ordered, steps, gradient, first_moment, second_moment)


def solution(mesh):
    fine = Mesh(
        mesh.devices.reshape(2, 4, 4, 2, 2, 2, 2),
        ("z_hi", "y", "x", "z_top", "z_mid", "z_lo", "core"),
    )
    dp, shard = ("z_hi", "y", "x"), ("z_top", "z_mid", "z_lo", "core")
    return jax.shard_map(
        per_device,
        mesh=fine,
        in_specs=(
            P(dp, None),
            P(None, dp, shard),
            P(None, dp, None),
            P(None, dp, shard),
            P(None, dp, shard),
        ),
        out_specs=(P(None, dp, shard), P(None, dp, shard), P(None, dp, shard)),
        check_vma=False,
    )
```

time: 126 us -> 111 us (0.88)
  the two profiles are of different devices: /device:TPU:1 before, /device:TPU:32 now
where the time goes in v2:
time: 111 us; the launch traced here: 110 us
  blocking collectives  55.9 us (50%)
  starting transfers between devices  33.2 us (30%)
  waiting for transfers between devices  12.6 us (11%)
  Pallas kernels  3.63 us (3%)
  local copies, waits for them, and re-layouts  3.39 us (3%)
    all_to_all x2, blocking collectives, spread(): lax.all_to_all(jnp.broadcast_to(block, (count, *block.shape)), axes, 0, 0...  43.9 us
    ppermute x1, starting transfers between devices, per_device(): lax.ppermute(mine, LINE, [(z, 15 - z) for z in (0, 1, 6, 7, 8, 9, 14, 15)])  11.4 us
    all_to_all x1, blocking collectives, per_device(): projected = lax.all_to_all(projected, NEAR, 0, 0, tiled=True)  9.79 us
    ppermute x1, starting transfers between devices, per_device(): moments_far = lax.ppermute(moments, 'z_hi', SWAP)  9.1 us
    ppermute x1, starting transfers between devices, per_device(): far = lax.ppermute(own.astype(bf16), 'z_hi', SWAP)  9.09 us
    all_to_all x1, waiting for transfers between devices, per_device(): parts = lax.all_to_all(partial, PLANE, 0, 0, tiled=True)  6.99 us
    ppermute x1, waiting for transfers between devices, per_device(): far = lax.ppermute(own.astype(bf16), 'z_hi', SWAP)  5.65 us
    all_to_all x1, starting transfers between devices, per_device(): parts = lax.all_to_all(partial, PLANE, 0, 0, tiled=True)  3.63 us
  transfers between devices with their start and end apart: 4, of which 2 were waited for; matrix products, arithmetic and copies ran while one was open for 0% of the time, Pallas kernels for 0%

profile of v2, /device:TPU:32, one launch (start us, length us, event | category | flops | bytes accessed | tf_op | source)
XLA Modules:
  0.0 110.5 jit_solution(11082888779656200930)
XLA Ops:
  0.6 0.0 copy-start
  0.7 0.1 dynamic_slice.12
  0.8 0.8 copy-done
  1.6 0.3 convolution_convert_fusion.1
  1.8 11.4 %collective-permute-start.1 = (bf16[256,128]{1,0:T(8,128)(2,1)S(1)}, bf16[256,128]{1,0:T(8,128)(2,1)S(1)}, u32[]{:S(2)}, u32[]{:S(2)}) collective-permute-start(bf16[256,128]{1,0:T(8,128)(2,1)S(1)} %convolution_convert_fusion.1), channel_id=1, source_target_pairs={{0,270},{2,268},{12,258},{14,256},{256,14},{258,12},{268,2},{270,0... | collective-permute-start | bytes 196616 | tf_op jit(solution)/shard_map/ppermute | solution.py:126
  13.3 2.2 %copy-done.1 = bf16[256,8192]{1,0:T(8,128)(2,1)S(1)} copy-done((bf16[256,8192]{1,0:T(8,128)(2,1)S(1)}, bf16[256,8192]{1,0:T(8,128)(2,1)}, u32[]{:S(2)}) %copy-start.1) | copy-done | bytes 4194328
  15.5 0.2 fetch.1.inputs_ref
  15.7 0.2 broadcast_in_dim.8
  15.9 23.7 %all_to_all.20.basis_ref = bf16[16,256,128]{2,1,0:T(8,128)(2,1)S(1)} all-to-all(bf16[16,256,128]{2,1,0:T(8,128)(2,1)S(1)} %broadcast_in_dim.8), channel_id=1, replica_groups=mesh['z_hi'=2,'y'=4,'x'=4,'z_top'=2,'z_mid'=2,'z_lo'=2,'core'=2] {'y','x'}, dimensions={0} | all-to-all | bytes 2097152 | tf_op jit(solution)/shard_map/all_to_all | solution.py:17
  39.6 0.8 project.1
  40.4 9.8 %all_to_all.21 = bf16[4,128,256]{2,1,0:T(8,128)(2,1)S(1)} all-to-all(bf16[4,128,256]{2,1,0:T(8,128)(2,1)S(1)} %project.1), channel_id=1, replica_groups=mesh['z_hi'=2,'y'=4,'x'=4,'z_top'=2,'z_mid'=2,'z_lo'=2,'core'=2] {'z_mid..., dimensions={0} | all-to-all | bytes 524288 | tf_op jit(solution)/shard_map/all_to_all | solution.py:138
  50.2 2.2 %all-gather = bf16[8,128,256]{2,1,0:T(8,128)(2,1)S(1)} all-gather(bf16[4,128,256]{2,1,0:T(8,128)(2,1)S(1)} %all_to_all.21), channel_id=2, replica_groups=mesh['z_hi'=2,'y'=4,'x'=4,'z_top'=2,'z_mid'=2,'z_lo'=2,'core'=2] {'core'}, dimensions={0}, use_global_device_ids=true | all-gather | bytes 786432 | tf_op jit(solution)/shard_map/all_gather | solution.py:139
  52.4 1.4 %gradient_parts.1 = bf16[16,2,16,896]{3,2,1,0:T(8,128)(2,1)} custom-call(bf16[2,2,256,256]{3,2,1,0:T(8,128)(2,1)S(1)} %bitcast.42, bf16[2,256,896]{2,1,0:T(8,128)(2,1)S(1)} %copy-done.2), custom_call_target="tpu_custom_call" | custom-call | tf_op jit(solution)/shard_map/gradient_parts/pallas_call | solution.py:24
  53.7 3.6 %all-to-all-start.2 = ((bf16[16,2,16,896]{3,2,1,0:T(8,128)(2,1)}), bf16[16,2,16,896]{3,2,1,0:T(8,128)(2,1)S(1)}, u32[]{:S(2)}, u32[]{:S(2)}) async-start(bf16[16,2,16,896]{3,2,1,0:T(8,128)(2,1)} %gradient_parts.1), calls=%async_computation.2 | async-start | bytes 1835008 | tf_op jit(solution)/shard_map/all_to_all | solution.py:147
  57.4 9.1 %collective-permute-start = (f32[2,2,8,896]{3,2,1,0:T(8,128)S(1)}, f32[2,2,8,896]{3,2,1,0:T(8,128)S(1)}, u32[]{:S(2)}, u32[]{:S(2)}) collective-permute-start(f32[2,2,8,896]{3,2,1,0:T(8,128)S(1)} %get-tuple-element.18), channel_id=1, source_target_pairs={{0,256},{256,0},{1,257},{257,1},{2,258},{258,2},{3,259},{259,3},{4... | collective-permute-start | bytes 344072 | tf_op jit(solution)/shard_map/ppermute | solution.py:128
  66.6 0.3 convolution_convert_fusion.basis_ref
  66.9 7.0 %all-to-all-done.2 = bf16[16,2,16,896]{3,2,1,0:T(8,128)(2,1)S(1)} async-done(((bf16[16,2,16,896]{3,2,1,0:T(8,128)(2,1)}), bf16[16,2,16,896]{3,2,1,0:T(8,128)(2,1)S(1)}, u32[]{:S(2)}, u32[]{:S(2)}) %all-to-all-start.2) | async-done | bytes 917536 | tf_op jit(solution)/shard_map/all_to_all | solution.py:147
  73.9 0.1 convert_reduce_fusion
  74.0 9.1 %collective-permute-start.2 = (bf16[2,2,8,896]{3,2,1,0:T(8,128)(2,1)S(1)}, bf16[2,2,8,896]{3,2,1,0:T(8,128)(2,1)S(1)}, u32[]{:S(2)}, u32[]{:S(2)}) collective-permute-start(bf16[2,2,8,896]{3,2,1,0:T(8,128)(2,1)S(1)} %bitcast_convert_fusion), channel_id=1, source_target_pairs={{0,256},{256,0},{1,257},{257,1},{2,258},{258,2},{3,259},{259,3},{4... | collective-permute-start | bytes 172040 | tf_op jit(solution)/shard_map/ppermute | solution.py:149
  83.2 5.7 %collective-permute-done.2 = bf16[2,2,8,896]{3,2,1,0:T(8,128)(2,1)S(1)} collective-permute-done((bf16[2,2,8,896]{3,2,1,0:T(8,128)(2,1)S(1)}, bf16[2,2,8,896]{3,2,1,0:T(8,128)(2,1)S(1)}, u32[]{:S(2)}, u32[]{:S(2)}) %collective-permute-start.2) | collective-permute-done | bytes 57376 | tf_op jit(solution)/shard_map/ppermute | solution.py:149
  88.8 0.1 fusion.16
  88.9 0.1 broadcast_in_dim.9
  89.0 20.2 %all_to_all.22.steps_ref = bf16[16,2,16,896]{3,2,1,0:T(8,128)(2,1)S(1)} all-to-all(bf16[16,2,16,896]{3,2,1,0:T(8,128)(2,1)S(1)} %broadcast_in_dim.9), channel_id=1, replica_groups=mesh['z_hi'=2,'y'=4,'x'=4,'z_top'=2,'z_mid'=2,'z_lo'=2,'core'=2] {'y','x'}, dimensions={0} | all-to-all | bytes 1835008 | tf_op jit(solution)/shard_map/all_to_all | solution.py:17
  109.2 1.3 %finish.1 = (bf16[2,256,896]{2,1,0:T(8,128)(2,1)}, f32[2,8,896]{2,1,0:T(8,128)}, f32[2,8,896]{2,1,0:T(8,128)}) custom-call(bf16[2,256,256]{2,1,0:T(8,128)(2,1)S(1)} %convolution_convert_fusion.basis_ref, bf16[16,2,16,896]{3,2,1,0:T(8,128)(2,1)S(1)} %all_to_all.22.steps_ref, f32[2,8,896]{2,1,0:T(8,128)S(1)} %dynamic-slice_bitcast_fusion.gradient_ref, ...), custom_call_target="tpu_custom_call" | custom-call | tf_op jit(solution)/shard_map/finish/pallas_call | solution.py:100
  (15 shorter events, 0.1 us)
Async XLA Ops:
  0.6 1.0 copy-start
  1.8 13.8 %collective-permute-start.1 = (bf16[256,128]{1,0:T(8,128)(2,1)S(1)}, bf16[256,128]{1,0:T(8,128)(2,1)S(1)}, u32[]{:S(2)}, u32[]{:S(2)}) collective-permute-start(bf16[256,128]{1,0:T(8,128)(2,1)S(1)} %convolution_convert_fusion.1), channel_id=1, source_target_pairs={{0,270},{2,268},{12,258},{14,256},{256,14},{258,12},{268,2},{270,0... | collective-permute-start | bytes 196616 | tf_op jit(solution)/shard_map/ppermute | solution.py:126
  13.3 2.2 %copy-start.1 = (bf16[256,8192]{1,0:T(8,128)(2,1)S(1)}, bf16[256,8192]{1,0:T(8,128)(2,1)}, u32[]{:S(2)}) copy-start(bf16[256,8192]{1,0:T(8,128)(2,1)} %inputs_ref.1) | copy-start | bytes 12582916
  39.6 12.7 %copy-start.2 = (bf16[2,256,896]{2,1,0:T(8,128)(2,1)S(1)}, bf16[2,256,896]{2,1,0:T(8,128)(2,1)}, u32[]{:S(2)}) copy-start(bf16[2,256,896]{2,1,0:T(8,128)(2,1)} %cotangent_ref.1) | copy-start | bytes 2752516
  52.4 5.0 %copy-start.3 = (f32[2,8,896]{2,1,0:T(8,128)S(1)}, f32[2,8,896]{2,1,0:T(8,128)}, u32[]{:S(2)}) copy-start(f32[2,8,896]{2,1,0:T(8,128)} %second_ref.1) | copy-start | bytes 172036
  52.4 5.0 %copy-start.4 = (f32[2,8,896]{2,1,0:T(8,128)S(1)}, f32[2,8,896]{2,1,0:T(8,128)}, u32[]{:S(2)}) copy-start(f32[2,8,896]{2,1,0:T(8,128)} %first_ref.1) | copy-start | bytes 172036
  53.7 20.1 %all-to-all-start.2 = ((bf16[16,2,16,896]{3,2,1,0:T(8,128)(2,1)}), bf16[16,2,16,896]{3,2,1,0:T(8,128)(2,1)S(1)}, u32[]{:S(2)}, u32[]{:S(2)}) async-start(bf16[16,2,16,896]{3,2,1,0:T(8,128)(2,1)} %gradient_parts.1), calls=%async_computation.2 | async-start | bytes 1835008 | tf_op jit(solution)/shard_map/all_to_all | solution.py:147
  57.4 25.7 %collective-permute-start = (f32[2,2,8,896]{3,2,1,0:T(8,128)S(1)}, f32[2,2,8,896]{3,2,1,0:T(8,128)S(1)}, u32[]{:S(2)}, u32[]{:S(2)}) collective-permute-start(f32[2,2,8,896]{3,2,1,0:T(8,128)S(1)} %get-tuple-element.18), channel_id=1, source_target_pairs={{0,256},{256,0},{1,257},{257,1},{2,258},{258,2},{3,259},{259,3},{4... | collective-permute-start | bytes 344072 | tf_op jit(solution)/shard_map/ppermute | solution.py:128
  74.0 14.8 %collective-permute-start.2 = (bf16[2,2,8,896]{3,2,1,0:T(8,128)(2,1)S(1)}, bf16[2,2,8,896]{3,2,1,0:T(8,128)(2,1)S(1)}, u32[]{:S(2)}, u32[]{:S(2)}) collective-permute-start(bf16[2,2,8,896]{3,2,1,0:T(8,128)(2,1)S(1)} %bitcast_convert_fusion), channel_id=1, source_target_pairs={{0,256},{256,0},{1,257},{257,1},{2,258},{258,2},{3,259},{259,3},{4... | collective-permute-start | bytes 172040 | tf_op jit(solution)/shard_map/ppermute | solution.py:149

commit v3 on v2

--- a/solution.py
+++ b/solution.py
@@ -64,11 +64,40 @@
     out_ref[...] = jnp.broadcast_to(acc.T.astype(bf16), (4, 128, 256))
 
 
-def gradient_kernel(halves_ref, cotangent_ref, out_ref):
+def gradient_kernel(halves_ref, cotangent_ref, out_ref, parts, sems):
+    copies = []
     for g in range(2):
         both = halves_ref[g, 0].astype(f32) + halves_ref[g, 1].astype(f32)
-        part = jnp.dot(both.astype(bf16), cotangent_ref[g], preferred_element_type=f32)
-        out_ref[:, g] = part.astype(bf16).reshape(16, 16, 896)
+        both = both.astype(bf16)
+        for piece in range(2):
+            rows = slice(piece * 8, piece * 8 + 8)
+            part = jnp.dot(
+                both[piece * 128 : piece * 128 + 128],
+                cotangent_ref[g],
+                preferred_element_type=f32,
+            )
+            parts[rows, g] = part.astype(bf16).reshape(8, 16, 896)
+            copies.append(
+                pltpu.make_async_copy(
+                    parts.at[rows, g], out_ref.at[rows, g], sems.at[2 * g + piece]
+                )
+            )
+            copies[-1].start()
+    for copy in copies:
+        copy.wait()
+
+
+def gradient_parts(halves, cotangent):
+    out = jax.ShapeDtypeStruct((16, 2, 16, 896), bf16)
+    return pl.pallas_call(
+        gradient_kernel,
+        in_specs=[pl.BlockSpec(memory_space=pltpu.VMEM)] * 2,
+        out_specs=pl.BlockSpec(memory_space=pl.ANY),
+        out_shape=out,
+        scratch_shapes=[pltpu.VMEM(out.shape, bf16), pltpu.SemaphoreType.DMA((4,))],
+        compiler_params=pltpu.CompilerParams(vmem_limit_bytes=16 * 2**20),
+        name="gradient_parts",
+    )(halves, cotangent)
 
 
 def update_kernel(basis_ref, steps_ref, gradient_ref, first_ref, second_ref, *refs):
@@ -77,16 +106,24 @@
     first[...] = 0.9 * first_ref[...] + 0.1 * gradient
     second[...] = 0.999 * second_ref[...] + 0.001 * gradient * gradient
     copies = [
-        pltpu.make_async_copy(first, outs[1], sems.at[2]),
-        pltpu.make_async_copy(second, outs[2], sems.at[3]),
+        pltpu.make_async_copy(first, outs[1], sems.at[4]),
+        pltpu.make_async_copy(second, outs[2], sems.at[5]),
     ]
     for copy in copies:
         copy.start()
     for g in range(2):
         steps = steps_ref[:, g].reshape(256, 896)
-        update[g] = jnp.dot(basis_ref[g], steps, preferred_element_type=f32).astype(bf16)
-        copies.append(pltpu.make_async_copy(update.at[g], outs[0].at[g], sems.at[g]))
-        copies[-1].start()
+        for piece in range(2):
+            rows = slice(piece * 128, piece * 128 + 128)
+            update[g, rows] = jnp.dot(
+                basis_ref[g, rows], steps, preferred_element_type=f32
+            ).astype(bf16)
+            copies.append(
+                pltpu.make_async_copy(
+                    update.at[g, rows], outs[0].at[g, rows], sems.at[2 * g + piece]
+                )
+            )
+            copies[-1].start()
     for copy in copies:
         copy.wait()
 
@@ -104,7 +141,7 @@
         out_shape=outs,
         scratch_shapes=[
             *(pltpu.VMEM(out.shape, out.dtype) for out in outs),
-            pltpu.SemaphoreType.DMA((4,)),
+            pltpu.SemaphoreType.DMA((6,)),
         ],
         compiler_params=pltpu.CompilerParams(vmem_limit_bytes=16 * 2**20),
         name="finish",
@@ -137,20 +174,15 @@
     )
     projected = lax.all_to_all(projected, NEAR, 0, 0, tiled=True)
     projected = lax.all_gather(projected, "core", axis=0).reshape(2, 2, 256, 256)
-    partial = in_vmem(
-        gradient_kernel,
-        jax.ShapeDtypeStruct((16, 2, 16, 896), bf16),
-        "gradient_parts",
-        projected,
-        cotangent,
-    )
+    partial = gradient_parts(projected, cotangent)
     parts = lax.all_to_all(partial, PLANE, 0, 0, tiled=True)
     own = jnp.sum(parts.astype(f32), axis=0).reshape(2, 2, 8, 896)
-    far = lax.ppermute(own.astype(bf16), "z_hi", SWAP)
+    sums = lax.all_gather(own.astype(bf16), "z_hi", axis=0)
+    sums, moments_far = lax.optimization_barrier((sums, moments_far))
     after, _ = lax.optimization_barrier((subspace, own))
     move = (order[:, None] == lax.broadcasted_iota(jnp.int32, (256, 256), 1)).astype(bf16)
     ordered = jnp.einsum("gdr,sr->gds", after, move, preferred_element_type=f32).astype(bf16)
-    gradient = own + far.astype(f32)
+    gradient = own + jnp.where(half == 0, sums[1], sums[0]).astype(f32)
 
     near_far = jnp.stack([moments, moments_far], axis=2)
     far_near = jnp.stack([moments_far, moments], axis=2)

time: 111 us -> 109 us (0.982)
  blocking collectives: 55.9 us -> 68.9 us
  starting transfers between devices: 33.2 us -> 24.1 us
  waiting for transfers between devices: 12.6 us -> 7.36 us
    all_gather x0 -> x1, blocking collectives: none -> 13.6 us  [per_device(): sums = lax.all_gather(own.astype(bf16), 'z_hi', axis=0)]
    ppermute x1 -> x0, starting transfers between devices: 9.09 us -> none  [per_device(): far = lax.ppermute(own.astype(bf16), 'z_hi', SWAP)]
    ppermute x1 -> x0, waiting for transfers between devices: 5.65 us -> none  [per_device(): far = lax.ppermute(own.astype(bf16), 'z_hi', SWAP)]
    pallas_call x2 -> x1, Pallas kernels: 2.14 us -> 0.78 us  [in_vmem(): pl.pallas_call(kernel, in_specs=[spec] * len(operands), out_specs=jax.tre...]
    pallas_call x0 -> x1, Pallas kernels: none -> 1.19 us  [gradient_parts(): pl.pallas_call(gradient_kernel, in_specs=[pl.BlockSpec(memory_space=pltpu...]
  transfers between devices with their start and end apart: 4 -> 3, of which waited for: 2 -> 1; matrix products, arithmetic and copies ran while one was open for 0% -> 0% of each run, Pallas kernels for 0% -> 0%
where the time goes in v3:
time: 109 us
  blocking collectives  68.9 us (63%)
  starting transfers between devices  24.1 us (22%)
  waiting for transfers between devices  7.36 us (7%)
  Pallas kernels  3.43 us (3%)
  local copies, waits for them, and re-layouts  3.38 us (3%)
    all_to_all x2, blocking collectives, spread(): lax.all_to_all(jnp.broadcast_to(block, (count, *block.shape)), axes, 0, 0...  43.4 us
    all_gather x1, blocking collectives, per_device(): sums = lax.all_gather(own.astype(bf16), 'z_hi', axis=0)  13.6 us
    ppermute x1, starting transfers between devices, per_device(): lax.ppermute(mine, LINE, [(z, 15 - z) for z in (0, 1, 6, 7, 8, 9, 14, 15)])  11.4 us
    all_to_all x1, blocking collectives, per_device(): projected = lax.all_to_all(projected, NEAR, 0, 0, tiled=True)  9.79 us
    ppermute x1, starting transfers between devices, per_device(): moments_far = lax.ppermute(moments, 'z_hi', SWAP)  9.1 us
    all_to_all x1, waiting for transfers between devices, per_device(): parts = lax.all_to_all(partial, PLANE, 0, 0, tiled=True)  7.35 us
    all_to_all x1, starting transfers between devices, per_device(): parts = lax.all_to_all(partial, PLANE, 0, 0, tiled=True)  3.65 us
    unnamed x10, local copies, waits for them, and re-layouts  3.04 us
  transfers between devices with their start and end apart: 3, of which 1 were waited for; matrix products, arithmetic and copies ran while one was open for 0% of the time, Pallas kernels for 0%

profile of v3, /device:TPU:32, one launch (start us, length us, event | category | flops | bytes accessed | tf_op | source)
XLA Modules:
  0.0 109.0 jit_solution(3190169198957797460)
XLA Ops:
  0.6 0.0 copy-start
  0.7 0.1 dynamic_slice.12
  0.8 0.8 copy-done
  1.6 0.3 convolution_convert_fusion.1
  1.8 11.4 %collective-permute-start = (bf16[256,128]{1,0:T(8,128)(2,1)S(1)}, bf16[256,128]{1,0:T(8,128)(2,1)S(1)}, u32[]{:S(2)}, u32[]{:S(2)}) collective-permute-start(bf16[256,128]{1,0:T(8,128)(2,1)S(1)} %convolution_convert_fusion.1), channel_id=1, source_target_pairs={{0,270},{2,268},{12,258},{14,256},{256,14},{258,12},{268,2},{270,0... | collective-permute-start | bytes 196616 | tf_op jit(solution)/shard_map/ppermute | solution.py:163
  13.3 0.0 copy-start.1
  13.3 2.2 %copy-done.1 = bf16[256,8192]{1,0:T(8,128)(2,1)S(1)} copy-done((bf16[256,8192]{1,0:T(8,128)(2,1)S(1)}, bf16[256,8192]{1,0:T(8,128)(2,1)}, u32[]{:S(2)}) %copy-start.1) | copy-done | bytes 4194328
  15.5 0.2 fetch.1.inputs_ref
  15.7 0.2 broadcast_in_dim.8
  15.9 23.7 %all_to_all.20.basis_ref = bf16[16,256,128]{2,1,0:T(8,128)(2,1)S(1)} all-to-all(bf16[16,256,128]{2,1,0:T(8,128)(2,1)S(1)} %broadcast_in_dim.8), channel_id=1, replica_groups=mesh['z_hi'=2,'y'=4,'x'=4,'z_top'=2,'z_mid'=2,'z_lo'=2,'core'=2] {'y','x'}, dimensions={0} | all-to-all | bytes 2097152 | tf_op jit(solution)/shard_map/all_to_all | solution.py:17
  39.6 0.8 project.1
  40.4 9.8 %all_to_all.21 = bf16[4,128,256]{2,1,0:T(8,128)(2,1)S(1)} all-to-all(bf16[4,128,256]{2,1,0:T(8,128)(2,1)S(1)} %project.1), channel_id=1, replica_groups=mesh['z_hi'=2,'y'=4,'x'=4,'z_top'=2,'z_mid'=2,'z_lo'=2,'core'=2] {'z_mid..., dimensions={0} | all-to-all | bytes 524288 | tf_op jit(solution)/shard_map/all_to_all | solution.py:175
  50.2 2.2 %all-gather = bf16[8,128,256]{2,1,0:T(8,128)(2,1)S(1)} all-gather(bf16[4,128,256]{2,1,0:T(8,128)(2,1)S(1)} %all_to_all.21), channel_id=2, replica_groups=mesh['z_hi'=2,'y'=4,'x'=4,'z_top'=2,'z_mid'=2,'z_lo'=2,'core'=2] {'core'}, dimensions={0}, use_global_device_ids=true | all-gather | bytes 786432 | tf_op jit(solution)/shard_map/all_gather | solution.py:176
  52.4 1.2 %gradient_parts.1 = bf16[16,2,16,896]{3,2,1,0:T(8,128)(2,1)} custom-call(bf16[2,2,256,256]{3,2,1,0:T(8,128)(2,1)S(1)} %bitcast.45, bf16[2,256,896]{2,1,0:T(8,128)(2,1)S(1)} %copy-done.2), custom_call_target="tpu_custom_call" | custom-call | tf_op jit(solution)/shard_map/gradient_parts/pallas_call | solution.py:92
  53.6 3.6 %all-to-all-start.2 = ((bf16[16,2,16,896]{3,2,1,0:T(8,128)(2,1)}), bf16[16,2,16,896]{3,2,1,0:T(8,128)(2,1)S(1)}, u32[]{:S(2)}, u32[]{:S(2)}) async-start(bf16[16,2,16,896]{3,2,1,0:T(8,128)(2,1)} %gradient_parts.1), calls=%async_computation.2 | async-start | bytes 1835008 | tf_op jit(solution)/shard_map/all_to_all | solution.py:178
  57.3 9.1 %collective-permute-start.1 = (f32[2,2,8,896]{3,2,1,0:T(8,128)S(1)}, f32[2,2,8,896]{3,2,1,0:T(8,128)S(1)}, u32[]{:S(2)}, u32[]{:S(2)}) collective-permute-start(f32[2,2,8,896]{3,2,1,0:T(8,128)S(1)} %get-tuple-element.20), channel_id=1, source_target_pairs={{0,256},{256,0},{1,257},{257,1},{2,258},{258,2},{3,259},{259,3},{4... | collective-permute-start | bytes 344072 | tf_op jit(solution)/shard_map/ppermute | solution.py:165
  66.4 7.4 %all-to-all-done.2 = bf16[16,2,16,896]{3,2,1,0:T(8,128)(2,1)S(1)} async-done(((bf16[16,2,16,896]{3,2,1,0:T(8,128)(2,1)}), bf16[16,2,16,896]{3,2,1,0:T(8,128)(2,1)S(1)}, u32[]{:S(2)}, u32[]{:S(2)}) %all-to-all-start.2) | async-done | bytes 917536 | tf_op jit(solution)/shard_map/all_to_all | solution.py:178
  73.7 0.1 convert_reduce_fusion
  73.9 13.6 %all_gather.12 = bf16[2,2,2,8,896]{4,3,2,1,0:T(8,128)(2,1)S(1)} all-gather(bf16[1,2,2,8,896]{4,3,2,1,0:T(8,128)(2,1)S(1)} %convert_bitcast_fusion.2), channel_id=1, replica_groups=mesh['z_hi'=2,'y'=4,'x'=4,'z_top'=2,'z_mid'=2,'z_lo'=2,'core'=2] {'z_hi'}, dimensions={0}, use_global_device_ids=true | all-gather | bytes 172032 | tf_op jit(solution)/shard_map/all_gather | solution.py:180
  87.5 0.1 fusion.15
  87.6 0.3 convolution_convert_fusion.basis_ref
  88.0 0.1 broadcast_in_dim.9
  88.1 19.7 %all_to_all.22.steps_ref = bf16[16,2,16,896]{3,2,1,0:T(8,128)(2,1)S(1)} all-to-all(bf16[16,2,16,896]{3,2,1,0:T(8,128)(2,1)S(1)} %broadcast_in_dim.9), channel_id=1, replica_groups=mesh['z_hi'=2,'y'=4,'x'=4,'z_top'=2,'z_mid'=2,'z_lo'=2,'core'=2] {'y','x'}, dimensions={0} | all-to-all | bytes 1835008 | tf_op jit(solution)/shard_map/all_to_all | solution.py:17
  107.7 1.2 %finish.1 = (bf16[2,256,896]{2,1,0:T(8,128)(2,1)}, f32[2,8,896]{2,1,0:T(8,128)}, f32[2,8,896]{2,1,0:T(8,128)}) custom-call(bf16[2,256,256]{2,1,0:T(8,128)(2,1)S(1)} %convolution_convert_fusion.basis_ref, bf16[16,2,16,896]{3,2,1,0:T(8,128)(2,1)S(1)} %all_to_all.22.steps_ref, f32[2,8,896]{2,1,0:T(8,128)S(1)} %fusion.17.gradient_ref, ...), custom_call_target="tpu_custom_call" | custom-call | tf_op jit(solution)/shard_map/finish/pallas_call | solution.py:137
  (15 shorter events, 0.1 us)
Async XLA Ops:
  0.6 1.0 copy-start
  1.8 13.8 %collective-permute-start = (bf16[256,128]{1,0:T(8,128)(2,1)S(1)}, bf16[256,128]{1,0:T(8,128)(2,1)S(1)}, u32[]{:S(2)}, u32[]{:S(2)}) collective-permute-start(bf16[256,128]{1,0:T(8,128)(2,1)S(1)} %convolution_convert_fusion.1), channel_id=1, source_target_pairs={{0,270},{2,268},{12,258},{14,256},{256,14},{258,12},{268,2},{270,0... | collective-permute-start | bytes 196616 | tf_op jit(solution)/shard_map/ppermute | solution.py:163
  13.3 2.2 %copy-start.1 = (bf16[256,8192]{1,0:T(8,128)(2,1)S(1)}, bf16[256,8192]{1,0:T(8,128)(2,1)}, u32[]{:S(2)}) copy-start(bf16[256,8192]{1,0:T(8,128)(2,1)} %inputs_ref.1) | copy-start | bytes 12582916
  39.6 12.7 %copy-start.2 = (bf16[2,256,896]{2,1,0:T(8,128)(2,1)S(1)}, bf16[2,256,896]{2,1,0:T(8,128)(2,1)}, u32[]{:S(2)}) copy-start(bf16[2,256,896]{2,1,0:T(8,128)(2,1)} %cotangent_ref.1) | copy-start | bytes 2752516
  52.4 4.9 %copy-start.3 = (f32[2,8,896]{2,1,0:T(8,128)S(1)}, f32[2,8,896]{2,1,0:T(8,128)}, u32[]{:S(2)}) copy-start(f32[2,8,896]{2,1,0:T(8,128)} %second_ref.1) | copy-start | bytes 172036
  52.4 4.9 %copy-start.4 = (f32[2,8,896]{2,1,0:T(8,128)S(1)}, f32[2,8,896]{2,1,0:T(8,128)}, u32[]{:S(2)}) copy-start(f32[2,8,896]{2,1,0:T(8,128)} %first_ref.1) | copy-start | bytes 172036
  53.6 20.2 %all-to-all-start.2 = ((bf16[16,2,16,896]{3,2,1,0:T(8,128)(2,1)}), bf16[16,2,16,896]{3,2,1,0:T(8,128)(2,1)S(1)}, u32[]{:S(2)}, u32[]{:S(2)}) async-start(bf16[16,2,16,896]{3,2,1,0:T(8,128)(2,1)} %gradient_parts.1), calls=%async_computation.2 | async-start | bytes 1835008 | tf_op jit(solution)/shard_map/all_to_all | solution.py:178
  57.3 30.2 %collective-permute-start.1 = (f32[2,2,8,896]{3,2,1,0:T(8,128)S(1)}, f32[2,2,8,896]{3,2,1,0:T(8,128)S(1)}, u32[]{:S(2)}, u32[]{:S(2)}) collective-permute-start(f32[2,2,8,896]{3,2,1,0:T(8,128)S(1)} %get-tuple-element.20), channel_id=1, source_target_pairs={{0,256},{256,0},{1,257},{257,1},{2,258},{258,2},{3,259},{259,3},{4... | collective-permute-start | bytes 344072 | tf_op jit(solution)/shard_map/ppermute | solution.py:165

commit v4 on v3

--- a/solution.py
+++ b/solution.py
@@ -162,7 +162,7 @@
     mine = jnp.einsum("dr,sr->ds", chosen, pick, preferred_element_type=f32).astype(bf16)
     theirs = lax.ppermute(mine, LINE, [(z, 15 - z) for z in (0, 1, 6, 7, 8, 9, 14, 15)])
     moments = jnp.stack([first_moment, second_moment])
-    moments_far = lax.ppermute(moments, "z_hi", SWAP)
+    moments_far = lax.ppermute(moments.astype(bf16), "z_hi", SWAP)
     features = jnp.where(across, 1 - half, half) * 4096
     held = fetch(inputs, features)
     basis = jnp.where(across, theirs, mine)
@@ -179,6 +179,7 @@
     own = jnp.sum(parts.astype(f32), axis=0).reshape(2, 2, 8, 896)
     sums = lax.all_gather(own.astype(bf16), "z_hi", axis=0)
     sums, moments_far = lax.optimization_barrier((sums, moments_far))
+    moments_far = moments_far.astype(f32)
     after, _ = lax.optimization_barrier((subspace, own))
     move = (order[:, None] == lax.broadcasted_iota(jnp.int32, (256, 256), 1)).astype(bf16)
     ordered = jnp.einsum("gdr,sr->gds", after, move, preferred_element_type=f32).astype(bf16)

time: 109 us -> 108 us (level)
  the two profiles are of different devices: /device:TPU:32 before, /device:TPU:2 now
where the time goes in v4:
time: 108 us
  blocking collectives  66.9 us (62%)
  starting transfers between devices  24.7 us (23%)
  waiting for transfers between devices  7.67 us (7%)
  Pallas kernels  3.42 us (3%)
  local copies, waits for them, and re-layouts  3.38 us (3%)
    all_to_all x2, blocking collectives, spread(): lax.all_to_all(jnp.broadcast_to(block, (count, *block.shape)), axes, 0, 0...  40.3 us
    all_gather x1, blocking collectives, per_device(): sums = lax.all_gather(own.astype(bf16), 'z_hi', axis=0)  14.2 us
    ppermute x1, starting transfers between devices, per_device(): lax.ppermute(mine, LINE, [(z, 15 - z) for z in (0, 1, 6, 7, 8, 9, 14, 15)])  11.4 us
    all_to_all x1, blocking collectives, per_device(): projected = lax.all_to_all(projected, NEAR, 0, 0, tiled=True)  10.2 us
    ppermute x1, starting transfers between devices, per_device(): moments_far = lax.ppermute(moments.astype(bf16), 'z_hi', SWAP)  8.4 us
    all_to_all x1, waiting for transfers between devices, per_device(): parts = lax.all_to_all(partial, PLANE, 0, 0, tiled=True)  6.63 us
    all_to_all x1, starting transfers between devices, per_device(): parts = lax.all_to_all(partial, PLANE, 0, 0, tiled=True)  4.88 us
    unnamed x10, local copies, waits for them, and re-layouts  3.04 us
  transfers between devices with their start and end apart: 3, of which 2 were waited for; matrix products, arithmetic and copies ran while one was open for 0% of the time, Pallas kernels for 0%

profile of v4, /device:TPU:2, one launch (start us, length us, event | category | flops | bytes accessed | tf_op | source)
XLA Modules:
  0.0 107.8 jit_solution(1087699595251106697)
XLA Ops:
  0.6 0.0 copy-start
  0.7 0.1 dynamic_slice.12
  0.8 0.8 copy-done
  1.6 0.3 convolution_convert_fusion.1
  1.8 11.4 %collective-permute-start = (bf16[256,128]{1,0:T(8,128)(2,1)S(1)}, bf16[256,128]{1,0:T(8,128)(2,1)S(1)}, u32[]{:S(2)}, u32[]{:S(2)}) collective-permute-start(bf16[256,128]{1,0:T(8,128)(2,1)S(1)} %convolution_convert_fusion.1), channel_id=1, source_target_pairs={{0,270},{2,268},{12,258},{14,256},{256,14},{258,12},{268,2},{270,0... | collective-permute-start | bytes 196616 | tf_op jit(solution)/shard_map/ppermute | solution.py:163
  13.3 2.2 %copy-done.1 = bf16[256,8192]{1,0:T(8,128)(2,1)S(1)} copy-done((bf16[256,8192]{1,0:T(8,128)(2,1)S(1)}, bf16[256,8192]{1,0:T(8,128)(2,1)}, u32[]{:S(2)}) %copy-start.1) | copy-done | bytes 4194328
  15.5 0.2 fetch.1.inputs_ref
  15.7 1.0 collective-permute-done
  16.8 0.2 broadcast_in_dim.8
  17.0 22.8 %all_to_all.20.basis_ref = bf16[16,256,128]{2,1,0:T(8,128)(2,1)S(1)} all-to-all(bf16[16,256,128]{2,1,0:T(8,128)(2,1)S(1)} %broadcast_in_dim.8), channel_id=1, replica_groups=mesh['z_hi'=2,'y'=4,'x'=4,'z_top'=2,'z_mid'=2,'z_lo'=2,'core'=2] {'y','x'}, dimensions={0} | all-to-all | bytes 2097152 | tf_op jit(solution)/shard_map/all_to_all | solution.py:17
  39.8 0.8 project.1
  40.6 10.2 %all_to_all.21 = bf16[4,128,256]{2,1,0:T(8,128)(2,1)S(1)} all-to-all(bf16[4,128,256]{2,1,0:T(8,128)(2,1)S(1)} %project.1), channel_id=1, replica_groups=mesh['z_hi'=2,'y'=4,'x'=4,'z_top'=2,'z_mid'=2,'z_lo'=2,'core'=2] {'z_mid..., dimensions={0} | all-to-all | bytes 524288 | tf_op jit(solution)/shard_map/all_to_all | solution.py:175
  50.8 2.2 %all-gather = bf16[8,128,256]{2,1,0:T(8,128)(2,1)S(1)} all-gather(bf16[4,128,256]{2,1,0:T(8,128)(2,1)S(1)} %all_to_all.21), channel_id=2, replica_groups=mesh['z_hi'=2,'y'=4,'x'=4,'z_top'=2,'z_mid'=2,'z_lo'=2,'core'=2] {'core'}, dimensions={0}, use_global_device_ids=true | all-gather | bytes 786432 | tf_op jit(solution)/shard_map/all_gather | solution.py:176
  53.0 1.2 %gradient_parts.1 = bf16[16,2,16,896]{3,2,1,0:T(8,128)(2,1)} custom-call(bf16[2,2,256,256]{3,2,1,0:T(8,128)(2,1)S(1)} %bitcast.47, bf16[2,256,896]{2,1,0:T(8,128)(2,1)S(1)} %copy-done.2), custom_call_target="tpu_custom_call" | custom-call | tf_op jit(solution)/shard_map/gradient_parts/pallas_call | solution.py:92
  54.2 4.9 %all-to-all-start.2 = ((bf16[16,2,16,896]{3,2,1,0:T(8,128)(2,1)}), bf16[16,2,16,896]{3,2,1,0:T(8,128)(2,1)S(1)}, u32[]{:S(2)}, u32[]{:S(2)}) async-start(bf16[16,2,16,896]{3,2,1,0:T(8,128)(2,1)} %gradient_parts.1), calls=%async_computation.2 | async-start | bytes 1835008 | tf_op jit(solution)/shard_map/all_to_all | solution.py:178
  59.1 8.4 %collective-permute-start.1 = (bf16[2,2,8,896]{3,2,1,0:T(8,128)(2,1)S(1)}, bf16[2,2,8,896]{3,2,1,0:T(8,128)(2,1)S(1)}, u32[]{:S(2)}, u32[]{:S(2)}) collective-permute-start(bf16[2,2,8,896]{3,2,1,0:T(8,128)(2,1)S(1)} %fusion.16), channel_id=1, source_target_pairs={{0,256},{256,0},{1,257},{257,1},{2,258},{258,2},{3,259},{259,3},{4... | collective-permute-start | bytes 172040 | tf_op jit(solution)/shard_map/ppermute | solution.py:165
  67.5 6.6 %all-to-all-done.2 = bf16[16,2,16,896]{3,2,1,0:T(8,128)(2,1)S(1)} async-done(((bf16[16,2,16,896]{3,2,1,0:T(8,128)(2,1)}), bf16[16,2,16,896]{3,2,1,0:T(8,128)(2,1)S(1)}, u32[]{:S(2)}, u32[]{:S(2)}) %all-to-all-start.2) | async-done | bytes 917536 | tf_op jit(solution)/shard_map/all_to_all | solution.py:178
  74.2 0.1 convert_reduce_fusion
  74.3 14.2 %all_gather.12 = bf16[2,2,2,8,896]{4,3,2,1,0:T(8,128)(2,1)S(1)} all-gather(bf16[1,2,2,8,896]{4,3,2,1,0:T(8,128)(2,1)S(1)} %convert_bitcast_fusion.2), channel_id=1, replica_groups=mesh['z_hi'=2,'y'=4,'x'=4,'z_top'=2,'z_mid'=2,'z_lo'=2,'core'=2] {'z_hi'}, dimensions={0}, use_global_device_ids=true | all-gather | bytes 172032 | tf_op jit(solution)/shard_map/all_gather | solution.py:180
  88.6 0.1 fusion.15
  88.7 0.3 convolution_convert_fusion.basis_ref
  89.0 0.1 broadcast_in_dim.9
  89.1 17.5 %all_to_all.22.steps_ref = bf16[16,2,16,896]{3,2,1,0:T(8,128)(2,1)S(1)} all-to-all(bf16[16,2,16,896]{3,2,1,0:T(8,128)(2,1)S(1)} %broadcast_in_dim.9), channel_id=1, replica_groups=mesh['z_hi'=2,'y'=4,'x'=4,'z_top'=2,'z_mid'=2,'z_lo'=2,'core'=2] {'y','x'}, dimensions={0} | all-to-all | bytes 1835008 | tf_op jit(solution)/shard_map/all_to_all | solution.py:17
  106.6 1.2 %finish.1 = (bf16[2,256,896]{2,1,0:T(8,128)(2,1)}, f32[2,8,896]{2,1,0:T(8,128)}, f32[2,8,896]{2,1,0:T(8,128)}) custom-call(bf16[2,256,256]{2,1,0:T(8,128)(2,1)S(1)} %convolution_convert_fusion.basis_ref, bf16[16,2,16,896]{3,2,1,0:T(8,128)(2,1)S(1)} %all_to_all.22.steps_ref, f32[2,8,896]{2,1,0:T(8,128)S(1)} %fusion.19.gradient_ref, ...), custom_call_target="tpu_custom_call" | custom-call | tf_op jit(solution)/shard_map/finish/pallas_call | solution.py:137
  (17 shorter events, 0.1 us)
Async XLA Ops:
  0.6 1.0 copy-start
  1.8 14.9 %collective-permute-start = (bf16[256,128]{1,0:T(8,128)(2,1)S(1)}, bf16[256,128]{1,0:T(8,128)(2,1)S(1)}, u32[]{:S(2)}, u32[]{:S(2)}) collective-permute-start(bf16[256,128]{1,0:T(8,128)(2,1)S(1)} %convolution_convert_fusion.1), channel_id=1, source_target_pairs={{0,270},{2,268},{12,258},{14,256},{256,14},{258,12},{268,2},{270,0... | collective-permute-start | bytes 196616 | tf_op jit(solution)/shard_map/ppermute | solution.py:163
  13.3 2.2 %copy-start.1 = (bf16[256,8192]{1,0:T(8,128)(2,1)S(1)}, bf16[256,8192]{1,0:T(8,128)(2,1)}, u32[]{:S(2)}) copy-start(bf16[256,8192]{1,0:T(8,128)(2,1)} %inputs_ref.1) | copy-start | bytes 12582916
  39.8 13.2 %copy-start.2 = (bf16[2,256,896]{2,1,0:T(8,128)(2,1)S(1)}, bf16[2,256,896]{2,1,0:T(8,128)(2,1)}, u32[]{:S(2)}) copy-start(bf16[2,256,896]{2,1,0:T(8,128)(2,1)} %cotangent_ref.1) | copy-start | bytes 2752516
  53.0 6.1 %copy-start.3 = (f32[2,8,896]{2,1,0:T(8,128)S(1)}, f32[2,8,896]{2,1,0:T(8,128)}, u32[]{:S(2)}) copy-start(f32[2,8,896]{2,1,0:T(8,128)} %second_ref.1) | copy-start | bytes 172036
  53.0 6.1 %copy-start.4 = (f32[2,8,896]{2,1,0:T(8,128)S(1)}, f32[2,8,896]{2,1,0:T(8,128)}, u32[]{:S(2)}) copy-start(f32[2,8,896]{2,1,0:T(8,128)} %first_ref.1) | copy-start | bytes 172036
  54.2 20.0 %all-to-all-start.2 = ((bf16[16,2,16,896]{3,2,1,0:T(8,128)(2,1)}), bf16[16,2,16,896]{3,2,1,0:T(8,128)(2,1)S(1)}, u32[]{:S(2)}, u32[]{:S(2)}) async-start(bf16[16,2,16,896]{3,2,1,0:T(8,128)(2,1)} %gradient_parts.1), calls=%async_computation.2 | async-start | bytes 1835008 | tf_op jit(solution)/shard_map/all_to_all | solution.py:178
  59.1 29.4 %collective-permute-start.1 = (bf16[2,2,8,896]{3,2,1,0:T(8,128)(2,1)S(1)}, bf16[2,2,8,896]{3,2,1,0:T(8,128)(2,1)S(1)}, u32[]{:S(2)}, u32[]{:S(2)}) collective-permute-start(bf16[2,2,8,896]{3,2,1,0:T(8,128)(2,1)S(1)} %fusion.16), channel_id=1, source_target_pairs={{0,256},{256,0},{1,257},{257,1},{2,258},{258,2},{3,259},{259,3},{4... | collective-permute-start | bytes 172040 | tf_op jit(solution)/shard_map/ppermute | solution.py:165

commit v5 on v4

--- a/solution.py
+++ b/solution.py
@@ -67,8 +67,7 @@
 def gradient_kernel(halves_ref, cotangent_ref, out_ref, parts, sems):
     copies = []
     for g in range(2):
-        both = halves_ref[g, 0].astype(f32) + halves_ref[g, 1].astype(f32)
-        both = both.astype(bf16)
+        both = halves_ref[g]
         for piece in range(2):
             rows = slice(piece * 8, piece * 8 + 8)
             part = jnp.dot(
@@ -173,7 +172,8 @@
         project_kernel, jax.ShapeDtypeStruct((4, 128, 256), bf16), "project", basis, held
     )
     projected = lax.all_to_all(projected, NEAR, 0, 0, tiled=True)
-    projected = lax.all_gather(projected, "core", axis=0).reshape(2, 2, 256, 256)
+    projected = jnp.sum(projected.reshape(2, 256, 256).astype(f32), axis=0).astype(bf16)
+    projected = lax.all_gather(projected, "core", axis=0)
     partial = gradient_parts(projected, cotangent)
     parts = lax.all_to_all(partial, PLANE, 0, 0, tiled=True)
     own = jnp.sum(parts.astype(f32), axis=0).reshape(2, 2, 8, 896)

time: 108 us -> 108 us (level)
  no operation moved by 1% of the time
where the time goes in v5:
time: 108 us
  blocking collectives  66.8 us (62%)
  starting transfers between devices  24.7 us (23%)
  waiting for transfers between devices  7.69 us (7%)
  Pallas kernels  3.42 us (3%)
  local copies, waits for them, and re-layouts  3.38 us (3%)
    all_to_all x2, blocking collectives, spread(): lax.all_to_all(jnp.broadcast_to(block, (count, *block.shape)), axes, 0, 0...  40.3 us
    all_gather x1, blocking collectives, per_device(): sums = lax.all_gather(own.astype(bf16), 'z_hi', axis=0)  14.2 us
    ppermute x1, starting transfers between devices, per_device(): lax.ppermute(mine, LINE, [(z, 15 - z) for z in (0, 1, 6, 7, 8, 9, 14, 15)])  11.4 us
    all_to_all x1, blocking collectives, per_device(): projected = lax.all_to_all(projected, NEAR, 0, 0, tiled=True)  10.2 us
    ppermute x1, starting transfers between devices, per_device(): moments_far = lax.ppermute(moments.astype(bf16), 'z_hi', SWAP)  8.4 us
    all_to_all x1, waiting for transfers between devices, per_device(): parts = lax.all_to_all(partial, PLANE, 0, 0, tiled=True)  6.65 us
    all_to_all x1, starting transfers between devices, per_device(): parts = lax.all_to_all(partial, PLANE, 0, 0, tiled=True)  4.9 us
    unnamed x10, local copies, waits for them, and re-layouts  3.04 us
  transfers between devices with their start and end apart: 3, of which 2 were waited for; matrix products, arithmetic and copies ran while one was open for 0% of the time, Pallas kernels for 0%

profile of v5, /device:TPU:2, one launch (start us, length us, event | category | flops | bytes accessed | tf_op | source)
XLA Modules:
  0.0 107.8 jit_solution(11102170510346828486)
XLA Ops:
  0.6 0.0 copy-start
  0.7 0.1 dynamic_slice.12
  0.8 0.8 copy-done
  1.6 0.3 convolution_convert_fusion.1
  1.8 11.4 %collective-permute-start = (bf16[256,128]{1,0:T(8,128)(2,1)S(1)}, bf16[256,128]{1,0:T(8,128)(2,1)S(1)}, u32[]{:S(2)}, u32[]{:S(2)}) collective-permute-start(bf16[256,128]{1,0:T(8,128)(2,1)S(1)} %convolution_convert_fusion.1), channel_id=1, source_target_pairs={{0,270},{2,268},{12,258},{14,256},{256,14},{258,12},{268,2},{270,0... | collective-permute-start | bytes 196616 | tf_op jit(solution)/shard_map/ppermute | solution.py:162
  13.3 2.2 %copy-done.1 = bf16[256,8192]{1,0:T(8,128)(2,1)S(1)} copy-done((bf16[256,8192]{1,0:T(8,128)(2,1)S(1)}, bf16[256,8192]{1,0:T(8,128)(2,1)}, u32[]{:S(2)}) %copy-start.1) | copy-done | bytes 4194328
  15.5 0.2 fetch.1.inputs_ref
  15.7 1.0 collective-permute-done
  16.8 0.2 broadcast_in_dim.8
  17.0 22.8 %all_to_all.20.basis_ref = bf16[16,256,128]{2,1,0:T(8,128)(2,1)S(1)} all-to-all(bf16[16,256,128]{2,1,0:T(8,128)(2,1)S(1)} %broadcast_in_dim.8), channel_id=1, replica_groups=mesh['z_hi'=2,'y'=4,'x'=4,'z_top'=2,'z_mid'=2,'z_lo'=2,'core'=2] {'y','x'}, dimensions={0} | all-to-all | bytes 2097152 | tf_op jit(solution)/shard_map/all_to_all | solution.py:17
  39.8 0.8 project.1
  40.6 10.2 %all_to_all.21 = bf16[4,128,256]{2,1,0:T(8,128)(2,1)S(1)} all-to-all(bf16[4,128,256]{2,1,0:T(8,128)(2,1)S(1)} %project.1), channel_id=1, replica_groups=mesh['z_hi'=2,'y'=4,'x'=4,'z_top'=2,'z_mid'=2,'z_lo'=2,'core'=2] {'z_mid..., dimensions={0} | all-to-all | bytes 524288 | tf_op jit(solution)/shard_map/all_to_all | solution.py:174
  50.8 2.1 %all-gather = bf16[512,256]{1,0:T(8,128)(2,1)S(1)} all-gather(bf16[256,256]{1,0:T(8,128)(2,1)S(1)} %bitcast_reduce_fusion), channel_id=2, replica_groups=mesh['z_hi'=2,'y'=4,'x'=4,'z_top'=2,'z_mid'=2,'z_lo'=2,'core'=2] {'core'}, dimensions={0}, use_global_device_ids=true | all-gather | bytes 393216 | tf_op jit(solution)/shard_map/all_gather | solution.py:176
  53.0 1.2 %gradient_parts.1 = bf16[16,2,16,896]{3,2,1,0:T(8,128)(2,1)} custom-call(bf16[2,256,256]{2,1,0:T(8,128)(2,1)S(1)} %bitcast.50, bf16[2,256,896]{2,1,0:T(8,128)(2,1)S(1)} %copy-done.2), custom_call_target="tpu_custom_call" | custom-call | tf_op jit(solution)/shard_map/gradient_parts/pallas_call | solution.py:91
  54.2 4.9 %all-to-all-start.2 = ((bf16[16,2,16,896]{3,2,1,0:T(8,128)(2,1)}), bf16[16,2,16,896]{3,2,1,0:T(8,128)(2,1)S(1)}, u32[]{:S(2)}, u32[]{:S(2)}) async-start(bf16[16,2,16,896]{3,2,1,0:T(8,128)(2,1)} %gradient_parts.1), calls=%async_computation.2 | async-start | bytes 1835008 | tf_op jit(solution)/shard_map/all_to_all | solution.py:178
  59.1 8.4 %collective-permute-start.1 = (bf16[2,2,8,896]{3,2,1,0:T(8,128)(2,1)S(1)}, bf16[2,2,8,896]{3,2,1,0:T(8,128)(2,1)S(1)}, u32[]{:S(2)}, u32[]{:S(2)}) collective-permute-start(bf16[2,2,8,896]{3,2,1,0:T(8,128)(2,1)S(1)} %fusion.16), channel_id=1, source_target_pairs={{0,256},{256,0},{1,257},{257,1},{2,258},{258,2},{3,259},{259,3},{4... | collective-permute-start | bytes 172040 | tf_op jit(solution)/shard_map/ppermute | solution.py:164
  67.5 6.6 %all-to-all-done.2 = bf16[16,2,16,896]{3,2,1,0:T(8,128)(2,1)S(1)} async-done(((bf16[16,2,16,896]{3,2,1,0:T(8,128)(2,1)}), bf16[16,2,16,896]{3,2,1,0:T(8,128)(2,1)S(1)}, u32[]{:S(2)}, u32[]{:S(2)}) %all-to-all-start.2) | async-done | bytes 917536 | tf_op jit(solution)/shard_map/all_to_all | solution.py:178
  74.2 0.1 convert_reduce_fusion
  74.3 14.2 %all_gather.12 = bf16[2,2,2,8,896]{4,3,2,1,0:T(8,128)(2,1)S(1)} all-gather(bf16[1,2,2,8,896]{4,3,2,1,0:T(8,128)(2,1)S(1)} %convert_bitcast_fusion.2), channel_id=1, replica_groups=mesh['z_hi'=2,'y'=4,'x'=4,'z_top'=2,'z_mid'=2,'z_lo'=2,'core'=2] {'z_hi'}, dimensions={0}, use_global_device_ids=true | all-gather | bytes 172032 | tf_op jit(solution)/shard_map/all_gather | solution.py:180
  88.6 0.1 fusion.15
  88.7 0.3 convolution_convert_fusion.basis_ref
  89.1 0.1 broadcast_in_dim.9
  89.1 17.5 %all_to_all.22.steps_ref = bf16[16,2,16,896]{3,2,1,0:T(8,128)(2,1)S(1)} all-to-all(bf16[16,2,16,896]{3,2,1,0:T(8,128)(2,1)S(1)} %broadcast_in_dim.9), channel_id=1, replica_groups=mesh['z_hi'=2,'y'=4,'x'=4,'z_top'=2,'z_mid'=2,'z_lo'=2,'core'=2] {'y','x'}, dimensions={0} | all-to-all | bytes 1835008 | tf_op jit(solution)/shard_map/all_to_all | solution.py:17
  106.6 1.2 %finish.1 = (bf16[2,256,896]{2,1,0:T(8,128)(2,1)}, f32[2,8,896]{2,1,0:T(8,128)}, f32[2,8,896]{2,1,0:T(8,128)}) custom-call(bf16[2,256,256]{2,1,0:T(8,128)(2,1)S(1)} %convolution_convert_fusion.basis_ref, bf16[16,2,16,896]{3,2,1,0:T(8,128)(2,1)S(1)} %all_to_all.22.steps_ref, f32[2,8,896]{2,1,0:T(8,128)S(1)} %fusion.19.gradient_ref, ...), custom_call_target="tpu_custom_call" | custom-call | tf_op jit(solution)/shard_map/finish/pallas_call | solution.py:136
  (18 shorter events, 0.2 us)
Async XLA Ops:
  0.6 1.0 copy-start
  1.8 14.9 %collective-permute-start = (bf16[256,128]{1,0:T(8,128)(2,1)S(1)}, bf16[256,128]{1,0:T(8,128)(2,1)S(1)}, u32[]{:S(2)}, u32[]{:S(2)}) collective-permute-start(bf16[256,128]{1,0:T(8,128)(2,1)S(1)} %convolution_convert_fusion.1), channel_id=1, source_target_pairs={{0,270},{2,268},{12,258},{14,256},{256,14},{258,12},{268,2},{270,0... | collective-permute-start | bytes 196616 | tf_op jit(solution)/shard_map/ppermute | solution.py:162
  13.3 2.2 %copy-start.1 = (bf16[256,8192]{1,0:T(8,128)(2,1)S(1)}, bf16[256,8192]{1,0:T(8,128)(2,1)}, u32[]{:S(2)}) copy-start(bf16[256,8192]{1,0:T(8,128)(2,1)} %inputs_ref.1) | copy-start | bytes 12582916
  39.8 13.2 %copy-start.2 = (bf16[2,256,896]{2,1,0:T(8,128)(2,1)S(1)}, bf16[2,256,896]{2,1,0:T(8,128)(2,1)}, u32[]{:S(2)}) copy-start(bf16[2,256,896]{2,1,0:T(8,128)(2,1)} %cotangent_ref.1) | copy-start | bytes 2752516
  50.8 8.3 %copy-start.3 = (f32[2,8,896]{2,1,0:T(8,128)S(1)}, f32[2,8,896]{2,1,0:T(8,128)}, u32[]{:S(2)}) copy-start(f32[2,8,896]{2,1,0:T(8,128)} %second_ref.1) | copy-start | bytes 172036
  50.8 8.2 %copy-start.4 = (f32[2,8,896]{2,1,0:T(8,128)S(1)}, f32[2,8,896]{2,1,0:T(8,128)}, u32[]{:S(2)}) copy-start(f32[2,8,896]{2,1,0:T(8,128)} %first_ref.1) | copy-start | bytes 172036
  54.2 20.0 %all-to-all-start.2 = ((bf16[16,2,16,896]{3,2,1,0:T(8,128)(2,1)}), bf16[16,2,16,896]{3,2,1,0:T(8,128)(2,1)S(1)}, u32[]{:S(2)}, u32[]{:S(2)}) async-start(bf16[16,2,16,896]{3,2,1,0:T(8,128)(2,1)} %gradient_parts.1), calls=%async_computation.2 | async-start | bytes 1835008 | tf_op jit(solution)/shard_map/all_to_all | solution.py:178
  59.1 29.4 %collective-permute-start.1 = (bf16[2,2,8,896]{3,2,1,0:T(8,128)(2,1)S(1)}, bf16[2,2,8,896]{3,2,1,0:T(8,128)(2,1)S(1)}, u32[]{:S(2)}, u32[]{:S(2)}) collective-permute-start(bf16[2,2,8,896]{3,2,1,0:T(8,128)(2,1)S(1)} %fusion.16), channel_id=1, source_target_pairs={{0,256},{256,0},{1,257},{257,1},{2,258},{258,2},{3,259},{259,3},{4... | collective-permute-start | bytes 172040 | tf_op jit(solution)/shard_map/ppermute | solution.py:164
